TPU v7x, 32 devices: a whole 2x2x4 slice. The times are simulated.
32 devices in a mesh: item: 4 (over y, core), user: 8 (over z, x).
Axes of the slice: x: 2, y: 2, z: 4, core: 2. Of those that a mesh axis runs over, the one named last changes fastest.
Arguments:
- item_factors: float32 [8192, 128], P('item')
- tile_lists: int32 [32, 16], P(('item', 'user')), may hold values from 0 to 63, as said below
- tile_weights: bfloat16 [32, 16, 128, 128], P(('item', 'user')), may hold values from 0 to 40
- user_factors: float32 [4096, 128], P(('item', 'user')), may hold values from -6 to 6
Outputs:
- new_factors: float32 [4096, 128], P(('item', 'user'))
Inputs may be any that keep to these rules, and one draw needn't show every extreme that they name: `tile_lists`: item shard s holds tiles s * 16 to (s + 1) * 16 - 1. Among the 16 slots of one device's blocks, at most 8 name tiles of one item shard, and for some shard exactly 8 do; a tile may be named more than once.
All inputs are finite; a program needn't handle non-finite values.
Results may differ from a plain program's by a relative error of at most 0.0024.
Values sent between devices are 32-bit elements; how exact they have to be, the bound alone decides.
A program may use at most 64 MiB of HBM per device.

v0:
```python
import jax
import jax.numpy as jnp
from jax import lax
from jax.sharding import PartitionSpec as P

ITERS = 4


RIDGE_WEIGHT = 0.1
EPSILON = 1e-06
HIGHEST = lax.Precision.HIGHEST


def apply_system(vectors, tiles, weights, gram):
    scores = jnp.einsum("bur,bkir->bkui", vectors, tiles, precision=HIGHEST)
    spread = jnp.einsum("bkui,bkir->bur", scores * weights, tiles, precision=HIGHEST)
    return (
        spread
        + jnp.einsum("bur,rs->bus", vectors, gram, precision=HIGHEST)
        + RIDGE_WEIGHT * vectors
    )


def conjugate(start, tiles, weights, gram, steps):
    weights = weights.astype(jnp.float32)
    target = jnp.einsum("bkui,bkir->bur", 1.0 + weights, tiles, precision=HIGHEST)
    answer = start
    resid = target - apply_system(start, tiles, weights, gram)
    direction = resid
    norm_now = jnp.sum(resid * resid, axis=-1, keepdims=True)
    for step_index in range(steps):
        image = apply_system(direction, tiles, weights, gram)
        alpha = norm_now / (jnp.sum(direction * image, axis=-1, keepdims=True) + EPSILON)
        answer = answer + alpha * direction
        resid = resid - alpha * image
        norm_next = jnp.sum(resid * resid, axis=-1, keepdims=True)
        direction = resid + norm_next / (norm_now + EPSILON) * direction
        norm_now = norm_next
    return answer


def local(item_factors, tile_lists, tile_weights, user_factors):
    factor_rank = item_factors.shape[1]
    tile_side = tile_weights.shape[-1]
    blocks_here, slots_here = tile_lists.shape
    partial_gram = jnp.dot(
        item_factors.T, item_factors, precision=HIGHEST, preferred_element_type=jnp.float32
    )
    gram = lax.psum(partial_gram, "item")
    tile_ids = tile_lists.reshape(-1)
    all_rows = lax.all_gather(item_factors, "item", axis=0, tiled=True)
    fetched = all_rows.reshape(-1, tile_side, factor_rank)[tile_ids]
    tiles = fetched.reshape(blocks_here, slots_here, tile_side, factor_rank)
    start = user_factors.reshape(blocks_here, tile_side, factor_rank)
    solved = conjugate(start, tiles, tile_weights, gram, ITERS)
    return solved.reshape(-1, factor_rank)


def solution(mesh):
    in_specs = (
        P("item", None),
        P(("item", "user"), None),
        P(("item", "user"), None, None, None),
        P(("item", "user"), None),
    )
    out_specs = P(("item", "user"), None)
    return jax.shard_map(local, mesh=mesh, in_specs=in_specs, out_specs=out_specs, check_vma=False)
```

profile of v0, /device:TPU:0, one launch (start us, length us, event | category | flops | bytes accessed | tf_op | source)
XLA Modules:
  0.0 101.3 jit_solution(11454904756243088005)
XLA Ops:
  6.5 0.0 copy-start.1
  6.5 0.0 all-gather.2.cloned.1.call-start
  6.5 0.7 all-gather.2.cloned.1.call-update
  7.3 0.0 all-reduce.2.cloned.1.call-start
  7.3 4.0 %fusion.24 = f32[128,128]{1,0:T(8,128)} fusion(f32[2048,128]{1,0:T(8,128)} %param.4), kind=kOutput, calls=%fused_computation.69 | convolution fusion | flops 402653184 | bytes 1114112 | tf_op jit(solution)/shard_map/dot_general | solution.py:46
  11.3 0.0 all-reduce.2.cloned.1.call-update
  11.4 0.7 fusion.22
  12.0 0.9 copy.33
  13.0 1.3 %copy.24 = bf16[1,16,128,128]{2,3,1,0:T(8,128)(2,1)S(1)} copy(bf16[1,16,128,128]{3,2,1,0:T(8,128)(2,1)} %param.6) | data formatting | bytes 1048576 | tf_op args[2]
  14.3 31.9 %all-gather.2.cloned.1.call-done = f32[8192,128]{1,0:T(8,128)} async-done(((f32[2048,128]{1,0:T(8,128)}), f32[8192,128]{1,0:T(8,128)}) %all-gather.2.cloned.1.call-update) | async-done | bytes 4194320 | tf_op jit(solution)/shard_map/all_gather | solution.py:51
  46.1 2.8 %gather_fusion = f32[16,128,128]{2,1,0:T(8,128)S(1)} fusion(f32[64,128,128]{2,1,0:T(8,128)} %bitcast.121, s32[1024]{0:T(1024)S(1)} %pad_clamp_fusion), kind=kCustom, calls=%fused_computation | custom fusion | bytes 2097216 | tf_op jit(solution)/shard_map/gather | solution.py:52
  48.9 0.0 copy-done.1
  49.0 1.0 fusion
  49.9 1.8 %convolution_bitcast_fusion.10 = f32[128,128]{0,1:T(8,128)S(1)} fusion(f32[16,128,128]{1,2,0:T(8,128)S(1)} %fusion, f32[16,128,128]{2,1,0:T(8,128)S(1)} %gather_fusion), kind=kOutput, calls=%fused_computation.34 | convolution fusion | flops 402653184 | bytes 2162688 | tf_op jit(solution)/shard_map/bkui,bkir->bur/dot_general | solution.py:16
  51.8 1.8 %convolution_bitcast_fusion.11 = f32[128,128]{0,1:T(8,128)S(1)} fusion(f32[16,128,128]{2,1,0:T(8,128)S(1)} %gather_fusion, bf16[1,16,128,128]{2,3,1,0:T(8,128)(2,1)S(1)} %copy.24), kind=kOutput, calls=%fused_computation.35 | convolution fusion | flops 403177472 | bytes 1638400 | tf_op jit(solution)/shard_map/bkui,bkir->bur/dot_general | solution.py:26
  53.6 26.0 %all-reduce.2.cloned.1.call-done = f32[128,128]{1,0:T(8,128)} async-done(((f32[128,128]{1,0:T(8,128)}), f32[128,128]{1,0:T(8,128)}) %all-reduce.2.cloned.1.call-update) | async-done | bytes 65552 | tf_op jit(solution)/shard_map/psum | solution.py:49
  79.5 0.0 copy-start
  79.6 1.2 %fusion.12 = f32[128,128]{0,1:T(8,128)S(1)} fusion(f32[128,128]{0,1:T(8,128)S(1)} %convolution_bitcast_fusion.11, f32[128,128]{0,1:T(8,128)S(1)} %convolution_bitcast_fusion.10, f32[128,128]{1,0:T(8,128)} %all-reduce.2.cloned.1.call-done, f32[128,128]{1,0:T(8,128)S(1)} %copy-done.1, f32[128,128]{0,1:T(8,128)S(1)} %copy.33), kind=kOutput, calls=%fused_computation.33 | convolution fusion | flops 25231360 | bytes 393216 | tf_op jit(solution)/shard_map/bur,rs->bus/dot_general | solution.py:19
  80.8 1.0 fusion.1
  81.7 1.8 %convolution_bitcast_fusion.8 = f32[128,128]{0,1:T(8,128)S(1)} fusion(f32[16,128,128]{1,2,0:T(8,128)S(1)} %fusion.1, f32[16,128,128]{2,1,0:T(8,128)S(1)} %gather_fusion), kind=kOutput, calls=%fused_computation.29 | convolution fusion | flops 402653184 | bytes 2162688 | tf_op jit(solution)/shard_map/bkui,bkir->bur/dot_general | solution.py:16
  83.6 0.0 copy-done
  83.6 0.3 multiply_reduce_fusion.5
  84.0 1.0 fusion.2
  84.9 2.0 %convolution_bitcast_fusion.7 = f32[128,128]{0,1:T(8,128)S(1)} fusion(f32[16,128,128]{1,2,0:T(8,128)S(1)} %fusion.2, f32[16,128,128]{2,1,0:T(8,128)S(1)} %gather_fusion), kind=kOutput, calls=%fused_computation.26 | convolution fusion | flops 402653184 | bytes 2162688 | tf_op jit(solution)/shard_map/bkui,bkir->bur/dot_general | solution.py:16
  86.9 0.3 multiply_reduce_fusion.3
  87.3 1.0 fusion.3
  88.3 1.8 %convolution_bitcast_fusion.6 = f32[128,128]{0,1:T(8,128)S(1)} fusion(f32[16,128,128]{1,2,0:T(8,128)S(1)} %fusion.3, f32[16,128,128]{2,1,0:T(8,128)S(1)} %gather_fusion), kind=kOutput, calls=%fused_computation.23 | convolution fusion | flops 402653184 | bytes 2162688 | tf_op jit(solution)/shard_map/bkui,bkir->bur/dot_general | solution.py:16
  90.1 0.3 multiply_reduce_fusion.1
  90.5 1.0 fusion.4
  91.5 1.8 %convolution_bitcast_fusion.5 = f32[128,128]{0,1:T(8,128)S(1)} fusion(f32[16,128,128]{1,2,0:T(8,128)S(1)} %fusion.4, f32[16,128,128]{2,1,0:T(8,128)S(1)} %gather_fusion), kind=kOutput, calls=%fused_computation.20 | convolution fusion | flops 402653184 | bytes 2162688 | tf_op jit(solution)/shard_map/bkui,bkir->bur/dot_general | solution.py:16
  93.3 0.3 fusion.13
  93.7 0.7 copy.43
  (15 shorter events, 0.3 us)
Async XLA Ops:
  6.5 42.4 %copy-start.1 = (f32[128,128]{1,0:T(8,128)S(1)}, f32[128,128]{1,0:T(8,128)}, u32[]{:S(2)}) copy-start(f32[128,128]{1,0:T(8,128)} %param.7) | copy-start | bytes 196612
  6.5 39.6 %all-gather.2.cloned.1.call-start = ((), (), s32[]{:S(2)}) async-start(), calls=%async_computation | async-start | bytes 5242880 | tf_op jit(solution)/shard_map/all_gather | solution.py:51
  7.3 72.3 %all-reduce.2.cloned.1.call-start = ((), (), s32[]{:S(2)}) async-start(), calls=%async_computation.1 | async-start | bytes 131072 | tf_op jit(solution)/shard_map/psum | solution.py:49
  79.5 4.0 %copy-start = (f32[128,128]{1,0:T(8,128)S(1)}, f32[128,128]{1,0:T(8,128)}, u32[]{:S(2)}) copy-start(f32[128,128]{1,0:T(8,128)} %all-reduce.2.cloned.1.call-done) | copy-start | bytes 196612
Sparse Core Ops, SparseCore 0:
  8.9 37.1 all-gather.1
  48.4 31.0 all-reduce.1
where the time goes:
time: 102 us; the launch traced here: 101 us
  waiting for transfers between devices  58.5 us (57%)
  matrix products  22.4 us (22%)
  between operations  13.5 us (13%)
  local copies, waits for them, and re-layouts  5.79 us (6%)
    all_gather x1, waiting for transfers between devices, local(): all_rows = lax.all_gather(item_factors, 'item', axis=0, tiled=True)  31.9 us
    psum x1, waiting for transfers between devices, local(): gram = lax.psum(partial_gram, 'item')  26 us
    dot_general x5, matrix products, apply_system(): jnp.einsum('bkui,bkir->bur', scores * weights, tiles, precision=HIGHEST)  9.28 us
    dot_general x5, matrix products, apply_system(): scores = jnp.einsum('bur,bkir->bkui', vectors, tiles, precision=HIGHEST)  4.87 us
    dot_general x1, matrix products, local(): jnp.dot(item_factors.T, item_factors, precision=HIGHEST, preferred_elemen...  4.02 us
    gather x1, local copies, waits for them, and re-layouts, local(): fetched = all_rows.reshape(-1, tile_side, factor_rank)[tile_ids]  2.8 us
    dot_general x5, matrix products, apply_system(): jnp.einsum('bur,rs->bus', vectors, gram, precision=HIGHEST)  2.42 us
    unnamed x6, local copies, waits for them, and re-layouts  2.26 us
  transfers between devices with their start and end apart: 2, of which 2 were waited for; matrix products, arithmetic and copies ran while one was open for 14% of the time, Pallas kernels for 0%

commit v1 on v0

v1 whole, which is shorter than its diff:
```python
import functools

import jax
import jax.numpy as jnp
from jax import lax
from jax.experimental import pallas as pl
from jax.experimental.pallas import tpu as pltpu
from jax.sharding import PartitionSpec as P

ITERS = 4
RIDGE_WEIGHT = 0.1
EPSILON = 1e-06
ROWS = 16
GROUP = 2
MESH = pl.DeviceIdType.MESH
F32 = jnp.float32
BF16 = jnp.bfloat16


def split(value):
    high = value.astype(BF16)
    low = (value - high.astype(F32)).astype(BF16)
    return high, low


def beside(value):
    return jnp.concatenate(split(value), axis=1)


def stacked(value):
    pair = beside(value)
    return jnp.concatenate([pair, pair], axis=0)


def dot(a, b):
    return jnp.dot(a, b, preferred_element_type=F32)


def fold_columns(value):
    half = value.shape[1] // 2
    return value[:, :half] + value[:, half:]


def fold_rows(value):
    half = value.shape[0] // 2
    return value[:half] + value[half:]


def kernel(items, stages, lists_ref, shard_ref, w_ref, u_ref, out_ref, *scratch):
    bufs = scratch[:stages]
    (w_vm, u_vm, w_t, y_hl, y_t, in_sem, own_sem, sib_send, sib_recv, y_send, y_recv,
     x_send, x_recv, f_send, f_recv) = scratch[stages:]
    tiles = shard_ref.shape[0]
    slots = w_ref.shape[0]
    rank = shard_ref.shape[2]
    ny = items // 2
    piece = ROWS // GROUP

    me = lax.axis_index("item")
    user = lax.axis_index("user")
    y, core = me // 2, lax.rem(me, 2)
    sibling = y * 2 + (1 - core)
    g = lax.rem(user, GROUP)
    peer = user - g + (1 - g)
    sib_id = (sibling, user)
    peer_id = (me, peer)

    w_copy = pltpu.make_async_copy(w_ref, w_vm, in_sem.at[0])
    u_copy = pltpu.make_async_copy(u_ref, u_vm, in_sem.at[1])
    w_copy.start()
    u_copy.start()

    def y_id(step):
        return (lax.rem(y + step, ny) * 2 + core, user)

    barrier = pltpu.get_barrier_semaphore()
    pl.semaphore_signal(barrier, inc=1, device_id=sib_id, device_id_type=MESH)
    pl.semaphore_signal(barrier, inc=1, device_id=peer_id, device_id_type=MESH)
    for step in range(1, ny):
        pl.semaphore_signal(barrier, inc=1, device_id=y_id(step), device_id_type=MESH)
    pl.semaphore_wait(barrier, 1 + ny)

    def remote(src, dst, send, recv, device):
        return pltpu.make_async_remote_copy(
            src_ref=src, dst_ref=dst, send_sem=send, recv_sem=recv,
            device_id=device, device_id_type=MESH)

    def region(m, shard, part=None):
        span = pl.ds(pl.multiple_of(shard * tiles, tiles), tiles)
        if part is None:
            return bufs[m].at[span]
        return bufs[m].at[span, pl.ds(pl.multiple_of(part * piece, piece), piece)]

    def far(step):
        return lax.rem(y + ny - step, ny) * 2 + core

    def far_sib(step):
        return lax.rem(y + ny - step, ny) * 2 + (1 - core)

    def y_copy(m, step):
        rows = pl.ds(pl.multiple_of(m * ROWS + g * piece, piece), piece)
        return remote(shard_ref.at[:, rows], region(m, me, g),
                      y_send.at[step - 1, m], y_recv.at[step - 1, m], y_id(step))

    def y_arrival(m, step):
        place = region(m, far(step), g)
        return remote(place, place, y_send.at[step - 1, m], y_recv.at[step - 1, m], y_id(step))

    def x_copy(m, step, part):
        place = region(m, far(step), part)
        return remote(place, place, x_send.at[step - 1, m], x_recv.at[step - 1, m], peer_id)

    def f_copy(m, step, which, shard, part):
        place = region(m, shard, part)
        return remote(place, place, f_send.at[step - 1, which, m], f_recv.at[step - 1, which, m], sib_id)

    def own_to_sib(m):
        return remote(shard_ref.at[:, pl.ds(m * ROWS, ROWS)], region(m, me),
                      sib_send.at[m], sib_recv.at[m], sib_id)

    def own_copy(m):
        return pltpu.make_async_copy(shard_ref.at[:, pl.ds(m * ROWS, ROWS)], region(m, me), own_sem.at[m])

    for m in range(stages):
        for step in range(1, ny):
            y_copy(m, step).start()
        own_to_sib(m).start()
        own_copy(m).start()

    w_copy.wait()
    for k in range(slots):
        turned = w_vm[k].astype(F32).T
        for m in range(stages):
            w_t[m, k * ROWS:(k + 1) * ROWS, :] = turned[m * ROWS:(m + 1) * ROWS]
    u_copy.wait()
    answer = u_vm[...].T
    start_pair = stacked(answer)

    def spread_of(m, rows_hl, columns_t, vectors):
        scores = fold_columns(dot(rows_hl, vectors))
        return dot(columns_t, beside(scores * w_t[m]))

    gram = jnp.zeros((2 * rank, 2 * rank), F32)
    first = jnp.zeros((2 * rank, 2 * rank), F32)
    target = jnp.zeros((2 * rank, 2 * rank), F32)
    for turn in range(stages + 2):
        if turn < stages:
            for step in range(1, ny):
                y_arrival(turn, step).wait_recv()
                x_copy(turn, step, g).start()
                f_copy(turn, step, 0, far(step), g).start()
        if 1 <= turn <= stages:
            for step in range(1, ny):
                x_copy(turn - 1, step, 1 - g).wait_recv()
                f_copy(turn - 1, step, 1, far(step), 1 - g).start()
        if turn >= 2:
            m = turn - 2
            own_copy(m).wait()
            place = region(m, sibling)
            remote(place, place, sib_send.at[m], sib_recv.at[m], sib_id).wait_recv()
            for step in range(1, ny):
                f_copy(m, step, 0, far_sib(step), g).wait_recv()
                f_copy(m, step, 1, far_sib(step), 1 - g).wait_recv()
            every = beside(bufs[m][...].reshape(-1, rank))
            gram += lax.dot_general(every, every, (((0,), (0,)), ((), ())), preferred_element_type=F32)
            rows = jnp.concatenate([bufs[m][lists_ref[0, k]] for k in range(slots)], axis=0)
            rows_hl = beside(rows)
            columns_t = jnp.concatenate(split(rows.T), axis=0)
            y_hl[m] = rows_hl
            y_t[m] = columns_t
            first += spread_of(m, rows_hl, columns_t, start_pair)
            weights = w_t[m].astype(BF16)
            target += dot(columns_t, jnp.concatenate([weights, jnp.ones_like(weights)], axis=1))

    gram_hl = beside(fold_rows(fold_columns(gram)))

    def finish(spread, vectors, pair):
        return fold_rows(fold_columns(spread)) + fold_columns(dot(gram_hl, pair)) + RIDGE_WEIGHT * vectors

    resid = fold_rows(fold_columns(target)) - finish(first, answer, start_pair)
    direction = resid
    norm_now = jnp.sum(resid * resid, axis=0, keepdims=True)
    for index in range(ITERS):
        pair = stacked(direction)
        spread = jnp.zeros((2 * rank, 2 * rank), F32)
        for m in range(stages):
            spread += spread_of(m, y_hl[m], y_t[m], pair)
        image = finish(spread, direction, pair)
        alpha = norm_now / (jnp.sum(direction * image, axis=0, keepdims=True) + EPSILON)
        answer = answer + alpha * direction
        if index + 1 < ITERS:
            resid = resid - alpha * image
            norm_next = jnp.sum(resid * resid, axis=0, keepdims=True)
            direction = resid + norm_next / (norm_now + EPSILON) * direction
            norm_now = norm_next
    out_ref[...] = answer.T

    for m in range(stages):
        own_to_sib(m).wait_send()
        for step in range(1, ny):
            y_copy(m, step).wait_send()
            x_copy(m, step, g).wait_send()
            f_copy(m, step, 0, far(step), g).wait_send()
            f_copy(m, step, 1, far(step), 1 - g).wait_send()


def local(items, item_factors, tile_lists, tile_weights, user_factors):
    rank = item_factors.shape[1]
    side = tile_weights.shape[-1]
    slots = tile_lists.shape[1]
    stages = side // ROWS
    far = items // 2 - 1
    shard = item_factors.reshape(-1, side, rank)
    tiles = shard.shape[0]
    dma = pltpu.SemaphoreType.DMA
    scratch = [pltpu.VMEM((items * tiles, ROWS, rank), F32) for _ in range(stages)]
    scratch += [
        pltpu.VMEM((slots, side, side), BF16),
        pltpu.VMEM((side, rank), F32),
        pltpu.VMEM((stages, slots * ROWS, side), F32),
        pltpu.VMEM((stages, slots * ROWS, 2 * rank), BF16),
        pltpu.VMEM((stages, 2 * rank, slots * ROWS), BF16),
        dma((2,)), dma((stages,)), dma((stages,)), dma((stages,)),
        dma((far, stages)), dma((far, stages)), dma((far, stages)), dma((far, stages)),
        dma((far, 2, stages)), dma((far, 2, stages)),
    ]
    hbm = pl.BlockSpec(memory_space=pl.ANY)
    return pl.pallas_call(
        functools.partial(kernel, items, stages),
        out_shape=jax.ShapeDtypeStruct((side, rank), F32),
        in_specs=[pl.BlockSpec(memory_space=pltpu.SMEM), hbm, hbm, hbm],
        out_specs=pl.BlockSpec(memory_space=pltpu.VMEM),
        scratch_shapes=scratch,
        compiler_params=pltpu.CompilerParams(
            collective_id=0, has_side_effects=True, vmem_limit_bytes=48 * 1024 * 1024),
        name="half_sweep",
    )(tile_lists, shard, tile_weights.reshape(slots, side, side), user_factors)


def solution(mesh):
    in_specs = (
        P("item", None),
        P(("item", "user"), None),
        P(("item", "user"), None, None, None),
        P(("item", "user"), None),
    )
    out_specs = P(("item", "user"), None)
    body = functools.partial(local, mesh.shape["item"])
    return jax.shard_map(body, mesh=mesh, in_specs=in_specs, out_specs=out_specs, check_vma=False)
```

time: 102 us -> 35.8 us (0.35)
  waiting for transfers between devices: 58.5 us -> 0 us
  Pallas kernels: 0 us -> 30.7 us
  matrix products: 22.4 us -> 0 us
  between operations: 13.5 us -> 0.01 us
  local copies, waits for them, and re-layouts: 5.79 us -> 4.39 us
    all_gather x1 -> x0, waiting for transfers between devices: 31.9 us -> none  [local(): all_rows = lax.all_gather(item_factors, 'item', axis=0, tiled=True)]
    pallas_call x0 -> x1, Pallas kernels: none -> 30.7 us  [local(): pl.pallas_call(functools.partial(kernel, items, stages), out_shape=jax.Sh...]
    psum x1 -> x0, waiting for transfers between devices: 26 us -> none  [local(): gram = lax.psum(partial_gram, 'item')]
    dot_general x17 -> x0, matrix products: 22.4 us -> none  [the longest x5 9.28 us: apply_system(): jnp.einsum('bkui,bkir->bur', scores * weights, tiles, precision=HIGHEST)]
    gather x1 -> x0, local copies, waits for them, and re-layouts: 2.8 us -> none  [local(): fetched = all_rows.reshape(-1, tile_side, factor_rank)[tile_ids]]
    unnamed x6 -> x9, local copies, waits for them, and re-layouts: 2.26 us -> 4.39 us
  transfers between devices with their start and end apart: 2 -> 0, of which waited for: 2 -> 0; matrix products, arithmetic and copies ran while one was open for 14% -> 0% of each run, Pallas kernels for 0% -> 0%
where the time goes in v1:
time: 35.8 us; the launch traced here: 35.1 us
  Pallas kernels  30.7 us (86%)
  local copies, waits for them, and re-layouts  4.39 us (12%)
    pallas_call x1, Pallas kernels, local(): pl.pallas_call(functools.partial(kernel, items, stages), out_shape=jax.Sh...  30.7 us
    unnamed x9, local copies, waits for them, and re-layouts  4.39 us

profile of v1, /device:TPU:0, one launch (start us, length us, event | category | flops | bytes accessed | tf_op | source)
XLA Modules:
  0.0 35.1 jit_solution(7658077078579252630)
XLA Ops:
  0.0 0.0 copy-start.3
  0.0 0.7 %copy-done.3 = s32[1,16]{1,0:T(1,128)S(1)} copy-done((s32[1,16]{1,0:T(1,128)S(1)}, s32[1,16]{1,0:T(1,128)}, u32[]{:S(2)}) %copy-start.3) | copy-done | bytes 88
  0.7 0.0 copy-start
  0.7 1.2 %copy-done = f32[2048,128]{1,0:T(8,128)S(1)} copy-done((f32[2048,128]{1,0:T(8,128)S(1)}, f32[2048,128]{1,0:T(8,128)}, u32[]{:S(2)}) %copy-start) | copy-done | bytes 1048600
  1.9 0.0 copy-start.1
  1.9 1.0 %copy-done.1 = bf16[1,16,128,128]{3,2,1,0:T(8,128)(2,1)S(1)} copy-done((bf16[1,16,128,128]{3,2,1,0:T(8,128)(2,1)S(1)}, bf16[1,16,128,128]{3,2,1,0:T(8,128)(2,1)}, u32[]{:S(2)}) %copy-start.1) | copy-done | bytes 524312
  2.9 0.0 copy-start.2
  2.9 0.8 %copy-done.2 = f32[128,128]{1,0:T(8,128)S(1)} copy-done((f32[128,128]{1,0:T(8,128)S(1)}, f32[128,128]{1,0:T(8,128)}, u32[]{:S(2)}) %copy-start.2) | copy-done | bytes 65560
  3.8 30.7 %half_sweep.1 = f32[128,128]{1,0:T(8,128)S(1)} custom-call(s32[1,16]{1,0:T(1,128)S(1)} %copy-done.3, f32[16,128,128]{2,1,0:T(8,128)S(1)} %bitcast.2, bf16[16,128,128]{2,1,0:T(8,128)(2,1)S(1)} %bitcast.3, f32[128,128]{1,0:T(8,128)S(1)} %copy-done.2), custom_call_target="tpu_custom_call" | custom-call | tf_op jit(solution)/shard_map/half_sweep/pallas_call | solution.py:228
  34.4 0.6 %copy.6 = f32[128,128]{1,0:T(8,128)} copy(f32[128,128]{1,0:T(8,128)S(1)} %half_sweep.1) | data formatting | bytes 131072
Async XLA Ops:
  0.0 0.7 %copy-start.3 = (s32[1,16]{1,0:T(1,128)S(1)}, s32[1,16]{1,0:T(1,128)}, u32[]{:S(2)}) copy-start(s32[1,16]{1,0:T(1,128)} %lists_ref.1) | copy-start | bytes 196
  0.7 1.2 %copy-start = (f32[2048,128]{1,0:T(8,128)S(1)}, f32[2048,128]{1,0:T(8,128)}, u32[]{:S(2)}) copy-start(f32[2048,128]{1,0:T(8,128)} %param.4) | copy-start | bytes 3145732
  1.9 1.0 %copy-start.1 = (bf16[1,16,128,128]{3,2,1,0:T(8,128)(2,1)S(1)}, bf16[1,16,128,128]{3,2,1,0:T(8,128)(2,1)}, u32[]{:S(2)}) copy-start(bf16[1,16,128,128]{3,2,1,0:T(8,128)(2,1)} %param.6) | copy-start | bytes 1572868
  2.9 0.8 %copy-start.2 = (f32[128,128]{1,0:T(8,128)S(1)}, f32[128,128]{1,0:T(8,128)}, u32[]{:S(2)}) copy-start(f32[128,128]{1,0:T(8,128)} %u_ref.1) | copy-start | bytes 196612

commit v2 on v1

--- a/solution.py
+++ b/solution.py
@@ -46,15 +46,17 @@
     return value[:half] + value[half:]
 
 
-def kernel(items, stages, lists_ref, shard_ref, w_ref, u_ref, out_ref, *scratch):
+def kernel(items, stages, lists_hbm, shard_ref, w_ref, u_ref, out_ref, *scratch):
     bufs = scratch[:stages]
-    (w_vm, u_vm, w_t, y_hl, y_t, in_sem, own_sem, sib_send, sib_recv, y_send, y_recv,
+    (lists_ref, w_vm, u_vm, w_t, y_hl, y_t, in_sem, own_sem, sib_send, sib_recv, y_send, y_recv,
      x_send, x_recv, f_send, f_recv) = scratch[stages:]
     tiles = shard_ref.shape[0]
     slots = w_ref.shape[0]
     rank = shard_ref.shape[2]
     ny = items // 2
     piece = ROWS // GROUP
+    part_rows = slots * ROWS
+    all_rows = stages * part_rows
 
     me = lax.axis_index("item")
     user = lax.axis_index("user")
@@ -67,8 +69,10 @@
 
     w_copy = pltpu.make_async_copy(w_ref, w_vm, in_sem.at[0])
     u_copy = pltpu.make_async_copy(u_ref, u_vm, in_sem.at[1])
+    lists_copy = pltpu.make_async_copy(lists_hbm, lists_ref, in_sem.at[2])
     w_copy.start()
     u_copy.start()
+    lists_copy.start()
 
     def y_id(step):
         return (lax.rem(y + step, ny) * 2 + core, user)
@@ -131,18 +135,14 @@
     for k in range(slots):
         turned = w_vm[k].astype(F32).T
         for m in range(stages):
-            w_t[m, k * ROWS:(k + 1) * ROWS, :] = turned[m * ROWS:(m + 1) * ROWS]
+            w_t[m * part_rows + k * ROWS:m * part_rows + (k + 1) * ROWS] = turned[m * ROWS:(m + 1) * ROWS]
     u_copy.wait()
+    lists_copy.wait()
     answer = u_vm[...].T
     start_pair = stacked(answer)
 
-    def spread_of(m, rows_hl, columns_t, vectors):
-        scores = fold_columns(dot(rows_hl, vectors))
-        return dot(columns_t, beside(scores * w_t[m]))
-
-    gram = jnp.zeros((2 * rank, 2 * rank), F32)
+    gram = jnp.zeros((rank, 2 * rank), F32)
     first = jnp.zeros((2 * rank, 2 * rank), F32)
-    target = jnp.zeros((2 * rank, 2 * rank), F32)
     for turn in range(stages + 2):
         if turn < stages:
             for step in range(1, ny):
@@ -161,31 +161,27 @@
             for step in range(1, ny):
                 f_copy(m, step, 0, far_sib(step), g).wait_recv()
                 f_copy(m, step, 1, far_sib(step), 1 - g).wait_recv()
-            every = beside(bufs[m][...].reshape(-1, rank))
-            gram += lax.dot_general(every, every, (((0,), (0,)), ((), ())), preferred_element_type=F32)
+            every, rest = split(bufs[m][...].reshape(-1, rank))
+            gram += lax.dot_general(
+                every, jnp.concatenate([every, rest], axis=1), (((0,), (0,)), ((), ())), preferred_element_type=F32)
             rows = jnp.concatenate([bufs[m][lists_ref[0, k]] for k in range(slots)], axis=0)
             rows_hl = beside(rows)
             columns_t = jnp.concatenate(split(rows.T), axis=0)
-            y_hl[m] = rows_hl
-            y_t[m] = columns_t
-            first += spread_of(m, rows_hl, columns_t, start_pair)
-            weights = w_t[m].astype(BF16)
-            target += dot(columns_t, jnp.concatenate([weights, jnp.ones_like(weights)], axis=1))
-
-    gram_hl = beside(fold_rows(fold_columns(gram)))
-
-    def finish(spread, vectors, pair):
-        return fold_rows(fold_columns(spread)) + fold_columns(dot(gram_hl, pair)) + RIDGE_WEIGHT * vectors
-
-    resid = fold_rows(fold_columns(target)) - finish(first, answer, start_pair)
+            span = slice(m * part_rows, (m + 1) * part_rows)
+            y_hl[span] = rows_hl
+            y_t[:, span] = columns_t
+            scores = fold_columns(dot(rows_hl, start_pair))
+            first += dot(columns_t, beside(1.0 + w_t[span] * (1.0 - scores)))
+
+    gram_hl = beside(gram[:, :rank] + gram[:, rank:] + gram[:, rank:].T)
+    y_hl[all_rows:] = gram_hl
+    resid = fold_rows(fold_columns(first)) - fold_columns(dot(gram_hl, start_pair)) - RIDGE_WEIGHT * answer
     direction = resid
     norm_now = jnp.sum(resid * resid, axis=0, keepdims=True)
     for index in range(ITERS):
-        pair = stacked(direction)
-        spread = jnp.zeros((2 * rank, 2 * rank), F32)
-        for m in range(stages):
-            spread += spread_of(m, y_hl[m], y_t[m], pair)
-        image = finish(spread, direction, pair)
+        scores = fold_columns(dot(y_hl[...], stacked(direction)))
+        spread = dot(y_t[...], beside(scores[:all_rows] * w_t[...]))
+        image = fold_rows(fold_columns(spread)) + scores[all_rows:] + RIDGE_WEIGHT * direction
         alpha = norm_now / (jnp.sum(direction * image, axis=0, keepdims=True) + EPSILON)
         answer = answer + alpha * direction
         if index + 1 < ITERS:
@@ -215,12 +211,13 @@
     dma = pltpu.SemaphoreType.DMA
     scratch = [pltpu.VMEM((items * tiles, ROWS, rank), F32) for _ in range(stages)]
     scratch += [
+        pltpu.SMEM(tile_lists.shape, jnp.int32),
         pltpu.VMEM((slots, side, side), BF16),
         pltpu.VMEM((side, rank), F32),
-        pltpu.VMEM((stages, slots * ROWS, side), F32),
-        pltpu.VMEM((stages, slots * ROWS, 2 * rank), BF16),
-        pltpu.VMEM((stages, 2 * rank, slots * ROWS), BF16),
-        dma((2,)), dma((stages,)), dma((stages,)), dma((stages,)),
+        pltpu.VMEM((slots * side, side), F32),
+        pltpu.VMEM((slots * side + rank, 2 * rank), BF16),
+        pltpu.VMEM((2 * rank, slots * side), BF16),
+        dma((3,)), dma((stages,)), dma((stages,)), dma((stages,)),
         dma((far, stages)), dma((far, stages)), dma((far, stages)), dma((far, stages)),
         dma((far, 2, stages)), dma((far, 2, stages)),
     ]
@@ -228,11 +225,11 @@
     return pl.pallas_call(
         functools.partial(kernel, items, stages),
         out_shape=jax.ShapeDtypeStruct((side, rank), F32),
-        in_specs=[pl.BlockSpec(memory_space=pltpu.SMEM), hbm, hbm, hbm],
+        in_specs=[hbm, hbm, hbm, hbm],
         out_specs=pl.BlockSpec(memory_space=pltpu.VMEM),
         scratch_shapes=scratch,
         compiler_params=pltpu.CompilerParams(
-            collective_id=0, has_side_effects=True, vmem_limit_bytes=48 * 1024 * 1024),
+            collective_id=0, has_side_effects=True, vmem_limit_bytes=63 * 1024 * 1024),
         name="half_sweep",
     )(tile_lists, shard, tile_weights.reshape(slots, side, side), user_factors)
 

time: 35.8 us -> 32.1 us (0.90)
  local copies, waits for them, and re-layouts: 4.39 us -> 1.47 us
  Pallas kernels: 30.7 us -> 30 us
    unnamed x9 -> x1, local copies, waits for them, and re-layouts: 4.39 us -> 1.47 us
    pallas_call x1, Pallas kernels: 30.7 us -> 30 us  [local(): pl.pallas_call(functools.partial(kernel, items, stages), out_shape=jax.Sh...]
where the time goes in v2:
time: 32.1 us; the launch traced here: 31.5 us
  Pallas kernels  30 us (93%)
  local copies, waits for them, and re-layouts  1.47 us (5%)
    pallas_call x1, Pallas kernels, local(): pl.pallas_call(functools.partial(kernel, items, stages), out_shape=jax.Sh...  30 us
    unnamed x1, local copies, waits for them, and re-layouts  1.47 us

profile of v2, /device:TPU:0, one launch (start us, length us, event | category | flops | bytes accessed | tf_op | source)
XLA Modules:
  0.0 31.5 jit_solution(4747311724987026298)
XLA Ops:
  0.0 30.0 %half_sweep.1 = f32[128,128]{1,0:T(8,128)} custom-call(s32[1,16]{1,0:T(1,128)} %lists_hbm.1, f32[16,128,128]{2,1,0:T(8,128)} %bitcast.2, bf16[16,128,128]{2,1,0:T(8,128)(2,1)} %bitcast.3, f32[128,128]{1,0:T(8,128)} %u_ref.1), custom_call_target="tpu_custom_call" | custom-call | tf_op jit(solution)/shard_map/half_sweep/pallas_call | solution.py:225
  30.0 1.5 %copy.6 = f32[128,128]{1,0:T(8,128)} copy(f32[128,128]{1,0:T(8,128)} %half_sweep.1) | data formatting | bytes 131072

commit v3 on v2

--- a/solution.py
+++ b/solution.py
@@ -11,7 +11,7 @@
 RIDGE_WEIGHT = 0.1
 EPSILON = 1e-06
 ROWS = 16
-GROUP = 2
+GROUP = 4
 MESH = pl.DeviceIdType.MESH
 F32 = jnp.float32
 BF16 = jnp.bfloat16
@@ -49,12 +49,12 @@
 def kernel(items, stages, lists_hbm, shard_ref, w_ref, u_ref, out_ref, *scratch):
     bufs = scratch[:stages]
     (lists_ref, w_vm, u_vm, w_t, y_hl, y_t, in_sem, own_sem, sib_send, sib_recv, y_send, y_recv,
-     x_send, x_recv, f_send, f_recv) = scratch[stages:]
+     g_send, g_recv, f_send, f_recv) = scratch[stages:]
     tiles = shard_ref.shape[0]
     slots = w_ref.shape[0]
     rank = shard_ref.shape[2]
     ny = items // 2
-    piece = ROWS // GROUP
+    piece = tiles // GROUP
     part_rows = slots * ROWS
     all_rows = stages * part_rows
 
@@ -63,9 +63,12 @@
     y, core = me // 2, lax.rem(me, 2)
     sibling = y * 2 + (1 - core)
     g = lax.rem(user, GROUP)
-    peer = user - g + (1 - g)
+    g_low, g_high = lax.rem(g, 2), g // 2
+    base = user - g
+    parts = [g, g_high * 2 + (1 - g_low), (1 - g_high) * 2 + g_low, (1 - g_high) * 2 + (1 - g_low)]
     sib_id = (sibling, user)
-    peer_id = (me, peer)
+    low_id = (me, base + parts[1])
+    high_id = (me, base + parts[2])
 
     w_copy = pltpu.make_async_copy(w_ref, w_vm, in_sem.at[0])
     u_copy = pltpu.make_async_copy(u_ref, u_vm, in_sem.at[1])
@@ -79,21 +82,25 @@
 
     barrier = pltpu.get_barrier_semaphore()
     pl.semaphore_signal(barrier, inc=1, device_id=sib_id, device_id_type=MESH)
-    pl.semaphore_signal(barrier, inc=1, device_id=peer_id, device_id_type=MESH)
+    pl.semaphore_signal(barrier, inc=1, device_id=low_id, device_id_type=MESH)
+    pl.semaphore_signal(barrier, inc=1, device_id=high_id, device_id_type=MESH)
     for step in range(1, ny):
         pl.semaphore_signal(barrier, inc=1, device_id=y_id(step), device_id_type=MESH)
-    pl.semaphore_wait(barrier, 1 + ny)
+    pl.semaphore_wait(barrier, 2 + ny)
 
     def remote(src, dst, send, recv, device):
         return pltpu.make_async_remote_copy(
             src_ref=src, dst_ref=dst, send_sem=send, recv_sem=recv,
             device_id=device, device_id_type=MESH)
 
-    def region(m, shard, part=None):
-        span = pl.ds(pl.multiple_of(shard * tiles, tiles), tiles)
+    def region(m, shard, part=None, half=None):
         if part is None:
-            return bufs[m].at[span]
-        return bufs[m].at[span, pl.ds(pl.multiple_of(part * piece, piece), piece)]
+            return bufs[m].at[pl.ds(pl.multiple_of(shard * tiles, tiles), tiles)]
+        first, count = shard * tiles + part * piece, piece
+        if half is not None:
+            count = piece // 2
+            first = first + half * count
+        return bufs[m].at[pl.ds(first, count)]
 
     def far(step):
         return lax.rem(y + ny - step, ny) * 2 + core
@@ -102,20 +109,21 @@
         return lax.rem(y + ny - step, ny) * 2 + (1 - core)
 
     def y_copy(m, step):
-        rows = pl.ds(pl.multiple_of(m * ROWS + g * piece, piece), piece)
-        return remote(shard_ref.at[:, rows], region(m, me, g),
+        mine = shard_ref.at[pl.ds(g * piece, piece), pl.ds(m * ROWS, ROWS)]
+        return remote(mine, region(m, me, g),
                       y_send.at[step - 1, m], y_recv.at[step - 1, m], y_id(step))
 
     def y_arrival(m, step):
         place = region(m, far(step), g)
         return remote(place, place, y_send.at[step - 1, m], y_recv.at[step - 1, m], y_id(step))
 
-    def x_copy(m, step, part):
-        place = region(m, far(step), part)
-        return remote(place, place, x_send.at[step - 1, m], x_recv.at[step - 1, m], peer_id)
-
-    def f_copy(m, step, which, shard, part):
-        place = region(m, shard, part)
+    def g_copy(m, step, kind, part):
+        place = region(m, far(step), part, None if kind < 2 else kind - 2)
+        return remote(place, place, g_send.at[step - 1, kind, m], g_recv.at[step - 1, kind, m],
+                      low_id if kind in (0, 3) else high_id)
+
+    def f_copy(m, step, which, shard):
+        place = region(m, shard, parts[which])
         return remote(place, place, f_send.at[step - 1, which, m], f_recv.at[step - 1, which, m], sib_id)
 
     def own_to_sib(m):
@@ -143,24 +151,37 @@
 
     gram = jnp.zeros((rank, 2 * rank), F32)
     first = jnp.zeros((2 * rank, 2 * rank), F32)
-    for turn in range(stages + 2):
+    for turn in range(stages + 3):
         if turn < stages:
-            for step in range(1, ny):
-                y_arrival(turn, step).wait_recv()
-                x_copy(turn, step, g).start()
-                f_copy(turn, step, 0, far(step), g).start()
-        if 1 <= turn <= stages:
-            for step in range(1, ny):
-                x_copy(turn - 1, step, 1 - g).wait_recv()
-                f_copy(turn - 1, step, 1, far(step), 1 - g).start()
-        if turn >= 2:
+            m = turn
+            for step in range(1, ny):
+                y_arrival(m, step).wait_recv()
+                g_copy(m, step, 0, parts[0]).start()
+                g_copy(m, step, 1, parts[0]).start()
+                f_copy(m, step, 0, far(step)).start()
+        if 1 <= turn < stages + 1:
+            m = turn - 1
+            for step in range(1, ny):
+                g_copy(m, step, 0, parts[1]).wait_recv()
+                g_copy(m, step, 2, parts[1]).start()
+                f_copy(m, step, 1, far(step)).start()
+                g_copy(m, step, 1, parts[2]).wait_recv()
+                g_copy(m, step, 3, parts[2]).start()
+                f_copy(m, step, 2, far(step)).start()
+        if 2 <= turn < stages + 2:
             m = turn - 2
+            for step in range(1, ny):
+                g_copy(m, step, 2, parts[3]).wait_recv()
+                g_copy(m, step, 3, parts[3]).wait_recv()
+                f_copy(m, step, 3, far(step)).start()
+        if turn >= 3:
+            m = turn - 3
             own_copy(m).wait()
             place = region(m, sibling)
             remote(place, place, sib_send.at[m], sib_recv.at[m], sib_id).wait_recv()
             for step in range(1, ny):
-                f_copy(m, step, 0, far_sib(step), g).wait_recv()
-                f_copy(m, step, 1, far_sib(step), 1 - g).wait_recv()
+                for which in range(4):
+                    f_copy(m, step, which, far_sib(step)).wait_recv()
             every, rest = split(bufs[m][...].reshape(-1, rank))
             gram += lax.dot_general(
                 every, jnp.concatenate([every, rest], axis=1), (((0,), (0,)), ((), ())), preferred_element_type=F32)
@@ -195,9 +216,9 @@
         own_to_sib(m).wait_send()
         for step in range(1, ny):
             y_copy(m, step).wait_send()
-            x_copy(m, step, g).wait_send()
-            f_copy(m, step, 0, far(step), g).wait_send()
-            f_copy(m, step, 1, far(step), 1 - g).wait_send()
+            for kind in range(4):
+                g_copy(m, step, kind, parts[(0, 0, 1, 2)[kind]]).wait_send()
+                f_copy(m, step, kind, far(step)).wait_send()
 
 
 def local(items, item_factors, tile_lists, tile_weights, user_factors):
@@ -218,8 +239,8 @@
         pltpu.VMEM((slots * side + rank, 2 * rank), BF16),
         pltpu.VMEM((2 * rank, slots * side), BF16),
         dma((3,)), dma((stages,)), dma((stages,)), dma((stages,)),
-        dma((far, stages)), dma((far, stages)), dma((far, stages)), dma((far, stages)),
-        dma((far, 2, stages)), dma((far, 2, stages)),
+        dma((far, stages)), dma((far, stages)), dma((far, 4, stages)), dma((far, 4, stages)),
+        dma((far, 4, stages)), dma((far, 4, stages)),
     ]
     hbm = pl.BlockSpec(memory_space=pl.ANY)
     return pl.pallas_call(

time: 32.1 us -> 34.7 us (1.081)
  Pallas kernels: 30 us -> 32.6 us
    pallas_call x1, Pallas kernels: 30 us -> 32.6 us  [local(): pl.pallas_call(functools.partial(kernel, items, stages), out_shape=jax.Sh...]
where the time goes in v3:
time: 34.7 us; the launch traced here: 34.1 us
  Pallas kernels  32.6 us (94%)
  local copies, waits for them, and re-layouts  1.47 us (4%)
    pallas_call x1, Pallas kernels, local(): pl.pallas_call(functools.partial(kernel, items, stages), out_shape=jax.Sh...  32.6 us
    unnamed x1, local copies, waits for them, and re-layouts  1.47 us

profile of v3, /device:TPU:0, one launch (start us, length us, event | category | flops | bytes accessed | tf_op | source)
XLA Modules:
  0.0 34.1 jit_solution(12051977929993752503)
XLA Ops:
  0.0 32.6 %half_sweep.1 = f32[128,128]{1,0:T(8,128)} custom-call(s32[1,16]{1,0:T(1,128)} %lists_hbm.1, f32[16,128,128]{2,1,0:T(8,128)} %bitcast.2, bf16[16,128,128]{2,1,0:T(8,128)(2,1)} %bitcast.3, f32[128,128]{1,0:T(8,128)} %u_ref.1), custom_call_target="tpu_custom_call" | custom-call | tf_op jit(solution)/shard_map/half_sweep/pallas_call | solution.py:246
  32.7 1.5 %copy.6 = f32[128,128]{1,0:T(8,128)} copy(f32[128,128]{1,0:T(8,128)} %half_sweep.1) | data formatting | bytes 131072

commit v4 on v2

--- a/solution.py
+++ b/solution.py
@@ -48,8 +48,8 @@
 
 def kernel(items, stages, lists_hbm, shard_ref, w_ref, u_ref, out_ref, *scratch):
     bufs = scratch[:stages]
-    (lists_ref, w_vm, u_vm, w_t, y_hl, y_t, in_sem, own_sem, sib_send, sib_recv, y_send, y_recv,
-     x_send, x_recv, f_send, f_recv) = scratch[stages:]
+    (lists_ref, w_vm, u_vm, w_t, y_hl, y_t, grams, in_sem, own_sem, sib_send, sib_recv, y_send, y_recv,
+     x_send, x_recv, f_send, f_recv, gs_sem, gy_send, gy_recv, gf_send, gf_recv) = scratch[stages:]
     tiles = shard_ref.shape[0]
     slots = w_ref.shape[0]
     rank = shard_ref.shape[2]
@@ -125,11 +125,26 @@
     def own_copy(m):
         return pltpu.make_async_copy(shard_ref.at[:, pl.ds(m * ROWS, ROWS)], region(m, me), own_sem.at[m])
 
+    def gram_copy(shard, send, recv, device):
+        return remote(grams.at[shard], grams.at[shard], send, recv, device)
+
     for m in range(stages):
         for step in range(1, ny):
             y_copy(m, step).start()
         own_to_sib(m).start()
         own_copy(m).start()
+
+    part = jnp.zeros((rank, 2 * rank), F32)
+    for m in range(stages):
+        own_copy(m).wait()
+        mine = bufs[m][pl.ds(pl.multiple_of(me * tiles, tiles), tiles)]
+        high, low = split(mine.reshape(-1, rank))
+        part += lax.dot_general(
+            high, jnp.concatenate([high, low], axis=1), (((0,), (0,)), ((), ())), preferred_element_type=F32)
+    grams[me] = part[:, :rank] + part[:, rank:] + part[:, rank:].T
+    gram_copy(me, gs_sem.at[0], gs_sem.at[1], sib_id).start()
+    for step in range(1, ny):
+        gram_copy(me, gy_send.at[step - 1], gy_recv.at[step - 1], y_id(step)).start()
 
     w_copy.wait()
     for k in range(slots):
@@ -141,7 +156,6 @@
     answer = u_vm[...].T
     start_pair = stacked(answer)
 
-    gram = jnp.zeros((rank, 2 * rank), F32)
     first = jnp.zeros((2 * rank, 2 * rank), F32)
     for turn in range(stages + 2):
         if turn < stages:
@@ -155,15 +169,11 @@
                 f_copy(turn - 1, step, 1, far(step), 1 - g).start()
         if turn >= 2:
             m = turn - 2
-            own_copy(m).wait()
             place = region(m, sibling)
             remote(place, place, sib_send.at[m], sib_recv.at[m], sib_id).wait_recv()
             for step in range(1, ny):
                 f_copy(m, step, 0, far_sib(step), g).wait_recv()
                 f_copy(m, step, 1, far_sib(step), 1 - g).wait_recv()
-            every, rest = split(bufs[m][...].reshape(-1, rank))
-            gram += lax.dot_general(
-                every, jnp.concatenate([every, rest], axis=1), (((0,), (0,)), ((), ())), preferred_element_type=F32)
             rows = jnp.concatenate([bufs[m][lists_ref[0, k]] for k in range(slots)], axis=0)
             rows_hl = beside(rows)
             columns_t = jnp.concatenate(split(rows.T), axis=0)
@@ -173,16 +183,27 @@
             scores = fold_columns(dot(rows_hl, start_pair))
             first += dot(columns_t, beside(1.0 + w_t[span] * (1.0 - scores)))
 
-    gram_hl = beside(gram[:, :rank] + gram[:, rank:] + gram[:, rank:].T)
+    for step in range(1, ny):
+        gram_copy(far(step), gy_send.at[step - 1], gy_recv.at[step - 1], y_id(step)).wait_recv()
+        gram_copy(far(step), gf_send.at[step - 1], gf_recv.at[step - 1], sib_id).start()
+    gram_copy(sibling, gs_sem.at[0], gs_sem.at[1], sib_id).wait_recv()
+    for step in range(1, ny):
+        gram_copy(far_sib(step), gf_send.at[step - 1], gf_recv.at[step - 1], sib_id).wait_recv()
+    gram_hl = beside(jnp.sum(grams[...], axis=0))
     y_hl[all_rows:] = gram_hl
     resid = fold_rows(fold_columns(first)) - fold_columns(dot(gram_hl, start_pair)) - RIDGE_WEIGHT * answer
     direction = resid
     norm_now = jnp.sum(resid * resid, axis=0, keepdims=True)
     for index in range(ITERS):
         scores = fold_columns(dot(y_hl[...], stacked(direction)))
-        spread = dot(y_t[...], beside(scores[:all_rows] * w_t[...]))
-        image = fold_rows(fold_columns(spread)) + scores[all_rows:] + RIDGE_WEIGHT * direction
-        alpha = norm_now / (jnp.sum(direction * image, axis=0, keepdims=True) + EPSILON)
+        weighted = scores[:all_rows] * w_t[...]
+        image = scores[all_rows:] + RIDGE_WEIGHT * direction
+        curve = jnp.zeros_like(norm_now)
+        if index + 1 < ITERS:
+            image += fold_rows(fold_columns(dot(y_t[...], beside(weighted))))
+        else:
+            curve = jnp.sum(weighted * scores[:all_rows], axis=0, keepdims=True)
+        alpha = norm_now / (curve + jnp.sum(direction * image, axis=0, keepdims=True) + EPSILON)
         answer = answer + alpha * direction
         if index + 1 < ITERS:
             resid = resid - alpha * image
@@ -191,6 +212,10 @@
             norm_now = norm_next
     out_ref[...] = answer.T
 
+    gram_copy(me, gs_sem.at[0], gs_sem.at[1], sib_id).wait_send()
+    for step in range(1, ny):
+        gram_copy(me, gy_send.at[step - 1], gy_recv.at[step - 1], y_id(step)).wait_send()
+        gram_copy(far(step), gf_send.at[step - 1], gf_recv.at[step - 1], sib_id).wait_send()
     for m in range(stages):
         own_to_sib(m).wait_send()
         for step in range(1, ny):
@@ -217,9 +242,11 @@
         pltpu.VMEM((slots * side, side), F32),
         pltpu.VMEM((slots * side + rank, 2 * rank), BF16),
         pltpu.VMEM((2 * rank, slots * side), BF16),
+        pltpu.VMEM((items, rank, rank), F32),
         dma((3,)), dma((stages,)), dma((stages,)), dma((stages,)),
         dma((far, stages)), dma((far, stages)), dma((far, stages)), dma((far, stages)),
         dma((far, 2, stages)), dma((far, 2, stages)),
+        dma((2,)), dma((far,)), dma((far,)), dma((far,)), dma((far,)),
     ]
     hbm = pl.BlockSpec(memory_space=pl.ANY)
     return pl.pallas_call(

time: 32.1 us -> 33.3 us (1.037); the launches traced: 31.5 us -> 33.1 us
  Pallas kernels: 30 us -> 31.6 us
    pallas_call x1, Pallas kernels: 30 us -> 31.6 us  [local(): pl.pallas_call(functools.partial(kernel, items, stages), out_shape=jax.Sh...]
where the time goes in v4:
time: 33.3 us; the launch traced here: 33.1 us
  Pallas kernels  31.6 us (95%)
  local copies, waits for them, and re-layouts  1.47 us (4%)
    pallas_call x1, Pallas kernels, local(): pl.pallas_call(functools.partial(kernel, items, stages), out_shape=jax.Sh...  31.6 us
    unnamed x1, local copies, waits for them, and re-layouts  1.47 us

profile of v4, /device:TPU:0, one launch (start us, length us, event | category | flops | bytes accessed | tf_op | source)
XLA Modules:
  0.0 33.1 jit_solution(16422134021645067087)
XLA Ops:
  0.0 31.6 %half_sweep.1 = f32[128,128]{1,0:T(8,128)} custom-call(s32[1,16]{1,0:T(1,128)} %lists_hbm.1, f32[16,128,128]{2,1,0:T(8,128)} %bitcast.2, bf16[16,128,128]{2,1,0:T(8,128)(2,1)} %bitcast.3, f32[128,128]{1,0:T(8,128)} %u_ref.1), custom_call_target="tpu_custom_call" | custom-call | tf_op jit(solution)/shard_map/half_sweep/pallas_call | solution.py:252
  31.7 1.5 %copy.6 = f32[128,128]{1,0:T(8,128)} copy(f32[128,128]{1,0:T(8,128)} %half_sweep.1) | data formatting | bytes 131072

commit v5 on v4

--- a/solution.py
+++ b/solution.py
@@ -47,9 +47,9 @@
 
 
 def kernel(items, stages, lists_hbm, shard_ref, w_ref, u_ref, out_ref, *scratch):
-    bufs = scratch[:stages]
-    (lists_ref, w_vm, u_vm, w_t, y_hl, y_t, grams, in_sem, own_sem, sib_send, sib_recv, y_send, y_recv,
-     x_send, x_recv, f_send, f_recv, gs_sem, gy_send, gy_recv, gf_send, gf_recv) = scratch[stages:]
+    bufs, packs, lands = scratch[:stages], scratch[stages:2 * stages], scratch[2 * stages:3 * stages]
+    (lists_ref, sib_lists, w_vm, u_vm, w_t, y_hl, y_t, grams, in_sem, own_sem, sib_send, sib_recv, y_send, y_recv,
+     x_send, x_recv, gs_sem, gy_send, gy_recv, gf_send, gf_recv, l_sem) = scratch[3 * stages:]
     tiles = shard_ref.shape[0]
     slots = w_ref.shape[0]
     rank = shard_ref.shape[2]
@@ -90,7 +90,7 @@
             device_id=device, device_id_type=MESH)
 
     def region(m, shard, part=None):
-        span = pl.ds(pl.multiple_of(shard * tiles, tiles), tiles)
+        span = pl.ds(pl.multiple_of(shard // 2 * tiles, tiles), tiles)
         if part is None:
             return bufs[m].at[span]
         return bufs[m].at[span, pl.ds(pl.multiple_of(part * piece, piece), piece)]
@@ -114,16 +114,17 @@
         place = region(m, far(step), part)
         return remote(place, place, x_send.at[step - 1, m], x_recv.at[step - 1, m], peer_id)
 
-    def f_copy(m, step, which, shard, part):
-        place = region(m, shard, part)
-        return remote(place, place, f_send.at[step - 1, which, m], f_recv.at[step - 1, which, m], sib_id)
-
-    def own_to_sib(m):
-        return remote(shard_ref.at[:, pl.ds(m * ROWS, ROWS)], region(m, me),
-                      sib_send.at[m], sib_recv.at[m], sib_id)
+    def f_copy(m):
+        return remote(packs[m], lands[m], sib_send.at[m], sib_recv.at[m], sib_id)
+
+    def place(tile):
+        return tile // (2 * tiles) * tiles + tile % tiles
 
     def own_copy(m):
         return pltpu.make_async_copy(shard_ref.at[:, pl.ds(m * ROWS, ROWS)], region(m, me), own_sem.at[m])
+
+    list_copy = remote(lists_hbm, sib_lists, l_sem.at[0], l_sem.at[1], sib_id)
+    list_copy.start()
 
     def gram_copy(shard, send, recv, device):
         return remote(grams.at[shard], grams.at[shard], send, recv, device)
@@ -131,13 +132,12 @@
     for m in range(stages):
         for step in range(1, ny):
             y_copy(m, step).start()
-        own_to_sib(m).start()
         own_copy(m).start()
 
     part = jnp.zeros((rank, 2 * rank), F32)
     for m in range(stages):
         own_copy(m).wait()
-        mine = bufs[m][pl.ds(pl.multiple_of(me * tiles, tiles), tiles)]
+        mine = bufs[m][pl.ds(pl.multiple_of(y * tiles, tiles), tiles)]
         high, low = split(mine.reshape(-1, rank))
         part += lax.dot_general(
             high, jnp.concatenate([high, low], axis=1), (((0,), (0,)), ((), ())), preferred_element_type=F32)
@@ -153,6 +153,10 @@
             w_t[m * part_rows + k * ROWS:m * part_rows + (k + 1) * ROWS] = turned[m * ROWS:(m + 1) * ROWS]
     u_copy.wait()
     lists_copy.wait()
+    list_copy.wait()
+    here = [place(lists_ref[0, k]) for k in range(slots)]
+    there = [place(sib_lists[0, k]) for k in range(slots)]
+    local = [lists_ref[0, k] // tiles % 2 == core for k in range(slots)]
     answer = u_vm[...].T
     start_pair = stacked(answer)
 
@@ -162,19 +166,17 @@
             for step in range(1, ny):
                 y_arrival(turn, step).wait_recv()
                 x_copy(turn, step, g).start()
-                f_copy(turn, step, 0, far(step), g).start()
         if 1 <= turn <= stages:
             for step in range(1, ny):
                 x_copy(turn - 1, step, 1 - g).wait_recv()
-                f_copy(turn - 1, step, 1, far(step), 1 - g).start()
+            for k in range(slots):
+                packs[turn - 1][k] = bufs[turn - 1][there[k]]
+            f_copy(turn - 1).start()
         if turn >= 2:
             m = turn - 2
-            place = region(m, sibling)
-            remote(place, place, sib_send.at[m], sib_recv.at[m], sib_id).wait_recv()
-            for step in range(1, ny):
-                f_copy(m, step, 0, far_sib(step), g).wait_recv()
-                f_copy(m, step, 1, far_sib(step), 1 - g).wait_recv()
-            rows = jnp.concatenate([bufs[m][lists_ref[0, k]] for k in range(slots)], axis=0)
+            f_copy(m).wait_recv()
+            rows = jnp.concatenate(
+                [jnp.where(local[k], bufs[m][here[k]], lands[m][k]) for k in range(slots)], axis=0)
             rows_hl = beside(rows)
             columns_t = jnp.concatenate(split(rows.T), axis=0)
             span = slice(m * part_rows, (m + 1) * part_rows)
@@ -217,12 +219,10 @@
         gram_copy(me, gy_send.at[step - 1], gy_recv.at[step - 1], y_id(step)).wait_send()
         gram_copy(far(step), gf_send.at[step - 1], gf_recv.at[step - 1], sib_id).wait_send()
     for m in range(stages):
-        own_to_sib(m).wait_send()
+        f_copy(m).wait_send()
         for step in range(1, ny):
             y_copy(m, step).wait_send()
             x_copy(m, step, g).wait_send()
-            f_copy(m, step, 0, far(step), g).wait_send()
-            f_copy(m, step, 1, far(step), 1 - g).wait_send()
 
 
 def local(items, item_factors, tile_lists, tile_weights, user_factors):
@@ -234,8 +234,10 @@
     shard = item_factors.reshape(-1, side, rank)
     tiles = shard.shape[0]
     dma = pltpu.SemaphoreType.DMA
-    scratch = [pltpu.VMEM((items * tiles, ROWS, rank), F32) for _ in range(stages)]
+    scratch = [pltpu.VMEM((items // 2 * tiles, ROWS, rank), F32) for _ in range(stages)]
+    scratch += [pltpu.VMEM((slots, ROWS, rank), F32) for _ in range(2 * stages)]
     scratch += [
+        pltpu.SMEM(tile_lists.shape, jnp.int32),
         pltpu.SMEM(tile_lists.shape, jnp.int32),
         pltpu.VMEM((slots, side, side), BF16),
         pltpu.VMEM((side, rank), F32),
@@ -245,8 +247,7 @@
         pltpu.VMEM((items, rank, rank), F32),
         dma((3,)), dma((stages,)), dma((stages,)), dma((stages,)),
         dma((far, stages)), dma((far, stages)), dma((far, stages)), dma((far, stages)),
-        dma((far, 2, stages)), dma((far, 2, stages)),
-        dma((2,)), dma((far,)), dma((far,)), dma((far,)), dma((far,)),
+        dma((2,)), dma((far,)), dma((far,)), dma((far,)), dma((far,)), dma((2,)),
     ]
     hbm = pl.BlockSpec(memory_space=pl.ANY)
     return pl.pallas_call(

time: 33.3 us -> 33 us (level)
  no operation moved by 1% of the time
where the time goes in v5:
time: 33 us; the launch traced here: 32.9 us
  Pallas kernels  31.4 us (95%)
  local copies, waits for them, and re-layouts  1.47 us (4%)
    pallas_call x1, Pallas kernels, local(): pl.pallas_call(functools.partial(kernel, items, stages), out_shape=jax.Sh...  31.4 us
    unnamed x1, local copies, waits for them, and re-layouts  1.47 us

profile of v5, /device:TPU:0, one launch (start us, length us, event | category | flops | bytes accessed | tf_op | source)
XLA Modules:
  0.0 32.9 jit_solution(13410109894172668974)
XLA Ops:
  0.0 31.4 %half_sweep.1 = f32[128,128]{1,0:T(8,128)} custom-call(s32[1,16]{1,0:T(1,128)} %lists_hbm.1, f32[16,128,128]{2,1,0:T(8,128)} %bitcast.2, bf16[16,128,128]{2,1,0:T(8,128)(2,1)} %bitcast.3, f32[128,128]{1,0:T(8,128)} %u_ref.1), custom_call_target="tpu_custom_call" | custom-call | tf_op jit(solution)/shard_map/half_sweep/pallas_call | solution.py:253
  31.4 1.5 %copy.6 = f32[128,128]{1,0:T(8,128)} copy(f32[128,128]{1,0:T(8,128)} %half_sweep.1) | data formatting | bytes 131072

commit v6 on v2

--- a/solution.py
+++ b/solution.py
@@ -180,9 +180,14 @@
     norm_now = jnp.sum(resid * resid, axis=0, keepdims=True)
     for index in range(ITERS):
         scores = fold_columns(dot(y_hl[...], stacked(direction)))
-        spread = dot(y_t[...], beside(scores[:all_rows] * w_t[...]))
-        image = fold_rows(fold_columns(spread)) + scores[all_rows:] + RIDGE_WEIGHT * direction
-        alpha = norm_now / (jnp.sum(direction * image, axis=0, keepdims=True) + EPSILON)
+        weighted = scores[:all_rows] * w_t[...]
+        image = scores[all_rows:] + RIDGE_WEIGHT * direction
+        curve = jnp.zeros_like(norm_now)
+        if index + 1 < ITERS:
+            image += fold_rows(fold_columns(dot(y_t[...], beside(weighted))))
+        else:
+            curve = jnp.sum(weighted * scores[:all_rows], axis=0, keepdims=True)
+        alpha = norm_now / (curve + jnp.sum(direction * image, axis=0, keepdims=True) + EPSILON)
         answer = answer + alpha * direction
         if index + 1 < ITERS:
             resid = resid - alpha * image

time: 32.1 us -> 32 us (level)
  the two profiles are of different devices: /device:TPU:0 before, /device:TPU:1 now
where the time goes in v6:
time: 32 us; the launch traced here: 31.9 us
  Pallas kernels  30.4 us (95%)
  local copies, waits for them, and re-layouts  1.47 us (5%)
    pallas_call x1, Pallas kernels, local(): pl.pallas_call(functools.partial(kernel, items, stages), out_shape=jax.Sh...  30.4 us
    unnamed x1, local copies, waits for them, and re-layouts  1.47 us

profile of v6, /device:TPU:1, one launch (start us, length us, event | category | flops | bytes accessed | tf_op | source)
XLA Modules:
  0.0 31.9 jit_solution(2477535997709546058)
XLA Ops:
  0.0 30.4 %half_sweep.1 = f32[128,128]{1,0:T(8,128)} custom-call(s32[1,16]{1,0:T(1,128)} %lists_hbm.1, f32[16,128,128]{2,1,0:T(8,128)} %bitcast.2, bf16[16,128,128]{2,1,0:T(8,128)(2,1)} %bitcast.3, f32[128,128]{1,0:T(8,128)} %u_ref.1), custom_call_target="tpu_custom_call" | custom-call | tf_op jit(solution)/shard_map/half_sweep/pallas_call | solution.py:230
  30.4 1.5 %copy.6 = f32[128,128]{1,0:T(8,128)} copy(f32[128,128]{1,0:T(8,128)} %half_sweep.1) | data formatting | bytes 131072
